TPU v7x, 32 devices: a whole 2x2x4 slice. The times are simulated.
32 devices in a mesh: ens: 2 (over x), lon: 16 (over z, y, core).
Axes of the slice: x: 2, y: 2, z: 4, core: 2. Of those that a mesh axis runs over, the one named last changes fastest.
Arguments:
- tracer: float32 [4, 256, 75, 256], P(None, 'lon', None, 'ens'), parts along dimension 3, may hold values from -6 to 6
- east_speed: float32 [256, 75, 256], P('lon', None, 'ens'), parts along dimension 2, may hold values from -0.25 to 0.25
- north_speed: float32 [256, 75, 256], P('lon', None, 'ens'), parts along dimension 2, may hold values from -0.25 to 0.25
- diffusivity: float32 [256, 75, 256], P('lon', None, 'ens'), parts along dimension 2, may hold values from 0.02 to 0.2
- mixing: float32 [256, 75, 256], P('lon', None, 'ens'), parts along dimension 2, may hold values from 0.05 to 5
- thickness: float32 [256, 75, 256], P('lon', None, 'ens'), parts along dimension 2, may hold values from 0.5 to 2
- depth_levels: int32 [256, 256], P('lon', 'ens'), parts along dimension 1, may hold values from 0 to 75
- air_flux: float32 [8, 4096], P('ens', 'lon'), parts along dimension 0, may hold values from -6 to 6
- margin_tile: int32 [32768, 1], P(('ens', 'lon')), parts along dimension 0, may hold values from 0 to 15; in each aligned block of 1024 rows (0 to 1023, 1024 to 2047, ...) at most 64 rows name the same one
- margin_source: int32 [32768], P(('ens', 'lon')), parts along dimension 0, may hold values from 0 to 255
- margin_cell: int32 [32768], P(('ens', 'lon')), parts along dimension 0, may hold values from 0 to 2047
- margin_weight: float32 [32768], P(('ens', 'lon')), parts along dimension 0, may hold values from 0.2 to 1
Outputs:
- tracer_next: float32 [4, 256, 75, 256], P(None, 'lon', None, 'ens'), parts along dimension 3
There are 2 independent parts, one for each index of `ens`. A program takes and returns all parts, laid end to end along the dimension named above; each array names one. Nothing has to cross between parts.
Inputs may be any that keep to these rules, and one draw needn't show every extreme that they name: `margin_tile`: the rows of one tile name each ocean tile at most 64 times.
All inputs are finite; a program needn't handle non-finite values.
Results may differ from a plain program's by a relative error of at most 0.00002.
Values sent between devices are 32-bit elements; how exact they have to be, the bound alone decides.
No kernel may reach another device: no remote copies, remote signals or barrier semaphores. Data moves between devices by JAX's collectives and lax.ppermute only.
A program may use at most 192 MiB of HBM per device.

v0:
```python
import jax
import jax.numpy as jnp
from jax import lax
from jax.sharding import PartitionSpec as P

CAP = 64


def padded_2(shard, sides, width):
    for axis, dim in sides:
        size, length = (lax.axis_size(axis), shard.shape[dim])
        up = [(i, (i + 1) % size) for i in range(size)]
        down = [(j, i) for i, j in up]
        last = lax.slice_in_dim(shard, length - width, length, axis=dim)
        leading = lax.slice_in_dim(shard, 0, width, axis=dim)
        before = lax.ppermute(last, axis, up)
        after = lax.ppermute(leading, axis, down)
        shard = jnp.concatenate([before, shard, after], axis=dim)
    return shard


def from_partner(block, axis, apart):
    count = lax.axis_size(axis)
    route = []
    for low in range(count):
        high = low | 1 << apart
        if high != low and high < count:
            route += [(low, high), (high, low)]
    return lax.ppermute(block, axis, route)


def face_flux(speed, kappa_near, kappa_far, open_face, near, far):
    return open_face * (
        jnp.maximum(speed, 0.0) * near
        + jnp.minimum(speed, 0.0) * far
        + 0.5 * (kappa_near + kappa_far) * (near - far)
    )


def mix_columns(stepped, mixing, thickness, wet_mask, surface):
    levels = stepped.shape[2]
    wet_below = jnp.concatenate([wet_mask[:, 1:], jnp.zeros_like(wet_mask[:, :1])], axis=1)
    thickness_below = jnp.concatenate([thickness[:, 1:], thickness[:, -1:]], axis=1)
    coupling = mixing * wet_below / (0.5 * (thickness + thickness_below))
    prior_coupling = jnp.zeros_like(thickness[:, 0])
    prior_gain = jnp.zeros_like(thickness[:, 0])
    prior_value = jnp.zeros_like(stepped[:, :, 0])
    gain_list = []
    value_list = []
    for level_index in range(levels):
        here_coupling = coupling[:, level_index]
        here_thickness = thickness[:, level_index]
        pivot_value = here_thickness + here_coupling + prior_coupling - prior_coupling * prior_gain
        right_side = here_thickness * stepped[:, :, level_index]
        if level_index == 0:
            right_side = right_side + wet_mask[:, 0] * surface
        prior_value = (right_side + prior_coupling * prior_value) / pivot_value
        prior_gain = here_coupling / pivot_value
        prior_coupling = here_coupling
        gain_list.append(prior_gain)
        value_list.append(prior_value)
    solved = [value_list[-1]]
    for level_index in range(levels - 2, -1, -1):
        solved.append(value_list[level_index] + gain_list[level_index] * solved[-1])
    return jnp.stack(solved[::-1], axis=2)


def shards(
    tracer,
    east_speed,
    north_speed,
    diffusivity,
    mixing,
    thickness,
    depth_levels,
    air_flux,
    margin_tile,
    margin_source,
    margin_cell,
    margin_weight,
):
    lon_cells, levels, lat_cells = east_speed.shape
    tracer_count = tracer.shape[0]
    cycle_size = lax.axis_size("lon")
    level_ids = jnp.arange(levels, dtype=jnp.int32)
    wet_mask = (level_ids[None, :, None] < depth_levels[:, None, :]).astype(jnp.float32)
    stacked = jnp.concatenate([tracer, east_speed[None], diffusivity[None], wet_mask[None]], axis=0)
    edges = jnp.concatenate([stacked[:, :1], stacked[:, -1:]], axis=1)
    edge_halo = padded_2(edges, (("lon", 1),), 1)
    padded = jnp.concatenate([edge_halo[:, :1], stacked, edge_halo[:, 3:]], axis=1)
    padded_speed = padded[tracer_count]
    padded_kappa = padded[tracer_count + 1]
    padded_wet = padded[tracer_count + 2]
    east_flux = face_flux(
        padded_speed[None, :-1],
        padded_kappa[None, :-1],
        padded_kappa[None, 1:],
        (padded_wet[:-1] * padded_wet[1:])[None],
        padded[:tracer_count, :-1],
        padded[:tracer_count, 1:],
    )
    zonal_change = east_flux[:, 1:] - east_flux[:, :-1]
    top_rows = jnp.concatenate(
        [
            tracer[:, :, :, -1],
            north_speed[None, :, :, -1],
            diffusivity[None, :, :, -1],
            wet_mask[None, :, :, -1],
        ],
        axis=0,
    )
    mirror = top_rows
    for bit_index in range(cycle_size.bit_length() - 1):
        mirror = from_partner(mirror, "lon", bit_index)
    mirror = jnp.flip(mirror, axis=1)
    fold_flux = face_flux(
        (0.5 * (north_speed[:, :, -1] - mirror[tracer_count]))[None],
        diffusivity[None, :, :, -1],
        mirror[tracer_count + 1][None],
        (wet_mask[:, :, -1] * mirror[tracer_count + 2])[None],
        tracer[:, :, :, -1],
        mirror[:tracer_count],
    )
    inner_flux = face_flux(
        north_speed[None, :, :, :-1],
        diffusivity[None, :, :, :-1],
        diffusivity[None, :, :, 1:],
        (wet_mask[:, :, :-1] * wet_mask[:, :, 1:])[None],
        tracer[:, :, :, :-1],
        tracer[:, :, :, 1:],
    )
    north_flux = jnp.concatenate([inner_flux, fold_flux[..., None]], axis=3)
    south_flux = jnp.concatenate([jnp.zeros_like(inner_flux[..., :1]), inner_flux], axis=3)
    stepped = tracer - zonal_change - (north_flux - south_flux)
    dest_tile = margin_tile[:, 0]
    payload = margin_weight[None, :] * jnp.take(air_flux, margin_source, axis=1)
    onehot = (dest_tile[:, None] == jnp.arange(cycle_size, dtype=jnp.int32)[None, :]).astype(
        jnp.int32
    )
    before = jnp.cumsum(onehot, axis=0) - onehot
    slot_index = jnp.sum(before * onehot, axis=1)
    position = dest_tile * CAP + slot_index
    values = jnp.zeros((tracer_count, cycle_size * CAP), jnp.float32).at[:, position].set(payload)
    cell_ids = jnp.zeros((1, cycle_size * CAP), jnp.int32).at[0, position].set(margin_cell)
    received, received_cells = (
        lax.all_to_all(values, "lon", split_axis=1, concat_axis=1, tiled=True),
        lax.all_to_all(cell_ids, "lon", split_axis=1, concat_axis=1, tiled=True),
    )
    surface = (
        jnp.zeros((tracer_count, lon_cells * lat_cells), jnp.float32)
        .at[:, received_cells[0]]
        .add(received)
    )
    surface = surface.reshape(tracer_count, lon_cells, lat_cells)
    return mix_columns(stepped, mixing, thickness, wet_mask, surface)


def solution(mesh):
    placed = (
        P(None, "lon", None, "ens"),
        P("lon", None, "ens"),
        P("lon", None, "ens"),
        P("lon", None, "ens"),
        P("lon", None, "ens"),
        P("lon", None, "ens"),
        P("lon", "ens"),
        P("ens", "lon"),
        P(("ens", "lon"), None),
        P(("ens", "lon")),
        P(("ens", "lon")),
        P(("ens", "lon")),
    )
    return jax.shard_map(
        shards, mesh=mesh, in_specs=placed, out_specs=P(None, "lon", None, "ens"), check_vma=False
    )
```

profile of v0, /device:TPU:0, one launch (start us, length us, event | category | flops | bytes accessed | tf_op | source)
XLA Modules:
  0.0 142.0 jit_solution(13267512229541679027)
XLA Ops:
  0.8 3.4 %pad_maximum_fusion.5 = (f32[7,1,75,128]{3,1,0,2:T(1,128)}, f32[7,1,75,128]{3,1,0,2:T(1,128)}) fusion(f32[1,16,75,128]{3,1,0,2:T(8,128)S(1)} %fusion.7, f32[1,16,75,128]{3,1,0,2:T(8,128)} %bitcast.2261, f32[1,16,75,128]{3,1,0,2:T(8,128)} %bitcast.2265, f32[4,16,75,128]{3,1,2,0:T(8,128)} %param.12), kind=kLoop, calls=%fused_computation.39 | loop fusion | flops 403200 | bytes 4838400 | tf_op jit(solution)/shard_map/slice | solution.py:88
  4.6 5.0 %collective-permute-start.1 = (f32[7,1,75,128]{3,1,0,2:T(1,128)}, f32[7,1,75,128]{3,1,0,2:T(1,128)}, u32[]{:S(2)}, u32[]{:S(2)}) collective-permute-start(f32[7,1,75,128]{3,1,0,2:T(1,128)} %get-tuple-element.198), channel_id=1, source_target_pairs={{1,0},{2,1},{3,2},{4,3},{5,4},{6,5},{7,6},{8,7},{9,8},{10,9},{11,1... | collective-permute-start | bytes 806408 | tf_op jit(solution)/shard_map/ppermute | solution.py:17
  9.7 2.1 %slice.825 = f32[4,16,75,1]{3,1,2,0:T(8,128)} slice(f32[4,16,75,128]{3,1,2,0:T(8,128)S(1)} %copy-done), slice={[0:4], [0:16], [0:75], [127:128]} | slice | bytes 38400 | tf_op jit(solution)/shard_map/slice | solution.py:105
  14.0 1.4 copy.27984
  15.3 2.7 %copy.27985 = f32[4,16,75,1]{2,1,0,3:T(8,128)S(1)} copy(f32[4,16,75,1]{3,1,2,0:T(8,128)} %slice.825) | data formatting | bytes 38400 | tf_op jit(solution)/shard_map/slice | solution.py:105
  18.0 1.4 copy.27987
  19.4 2.1 %slice.826 = f32[16,75,1]{2,0,1:T(8,128)} slice(f32[16,75,128]{2,0,1:T(8,128)} %param.14), slice={[0:16], [0:75], [127:128]} | slice | bytes 9600 | tf_op jit(solution)/shard_map/slice | solution.py:106
  23.6 4.5 %reduce-window.6 = s32[16,8,128]{2,1,0:T(8,128)S(1)} reduce-window(s32[16,8,128]{2,1,0:T(8,128)S(1)} %fusion.21, s32[]{:T(128)} %constant.11.clone.1), window={size=1x1x128 pad=0_0x0_0x127_0}, to_apply=%region_0.1 | reduce-window | flops 2080768 | bytes 131076 | tf_op jit(solution)/shard_map/reduce-window
  28.8 4.5 %scatter_custom_fusion.2 = s32[1024]{0:T(1024)S(1)} fusion(s32[1024]{0:T(1024)S(1)} %broadcast_select_fusion, s32[1024]{0:T(1024)} %param.22, s32[]{:T(128)} %constant.11.clone.1), kind=kCustom, calls=%fused_computation.739 | custom fusion | bytes 4608
  33.9 4.2 %all-to-all-start = ((s32[1,16,64]{2,0,1:T(1,128)}), s32[1,16,64]{2,0,1:T(1,128)}, u32[]{:S(2)}, u32[]{:S(2)}) async-start(s32[1,16,64]{2,0,1:T(1,128)} %bitcast.23), calls=%async_computation | async-start | bytes 16384 | tf_op jit(solution)/shard_map/all_to_all | solution.py:147
  38.1 1.6 %slice_bitcast_fusion.148 = (f32[16,128]{1,0:T(8,128)}, f32[16,128]{1,0:T(8,128)}, f32[16,128]{1,0:T(8,128)}, f32[16,128]{1,0:T(8,128)}, f32[16,128]{1,0:T(8,128...) fusion(f32[16,75,128]{2,0,1:T(8,128)} %param.17), kind=kLoop, calls=%fused_computation.730 | loop fusion | bytes 311296 | tf_op jit(solution)/shard_map/mul | solution.py:54
  53.7 2.7 %add_multiply_fusion.1 = f32[4,16,75,127]{3,1,0,2:T(8,128)} fusion(f32[16,75,127]{2,0,1:T(8,128)S(1)} %get-tuple-element.405, f32[16,75,127]{2,0,1:T(8,128)S(1)} %get-tuple-element.395, f32[16,75,127]{2,0,1:T(8,128)S(1)} %get-tuple-element.394, f32[16,75,127]{2,0,1:T(8,128)S(1)} %get-tuple-element.404, f32[4,16,75,128]{3,1,2,0:T(8,128)S(1)} %copy-done), kind=kLoop, calls=%fused_computation.11 | loop fusion | flops 4267200 | bytes 9811200 | tf_op jit(solution)/shard_map/mul | solution.py:33
  60.5 1.6 %collective-permute-start.3 = (f32[7,16,75]{2,1,0:T(8,128)}, f32[7,16,75]{2,1,0:T(8,128)}, u32[]{:S(2)}, u32[]{:S(2)}) collective-permute-start(f32[7,16,75]{2,1,0:T(8,128)} %collective-permute-done.2), channel_id=1, source_target_pairs={{0,2},{2,0},{1,3},{3,1},{4,6},{6,4},{5,7},{7,5},{8,10},{10,8},{9,1... | collective-permute-start | bytes 100808 | tf_op jit(solution)/shard_map/ppermute | solution.py:29
  62.6 2.4 %collective-permute-done.3 = f32[7,16,75]{2,1,0:T(8,128)} collective-permute-done((f32[7,16,75]{2,1,0:T(8,128)}, f32[7,16,75]{2,1,0:T(8,128)}, u32[]{:S(2)}, u32[]{:S(2)}) %collective-permute-start.3) | collective-permute-done | bytes 33632 | tf_op jit(solution)/shard_map/ppermute | solution.py:29
  65.1 1.5 %collective-permute-start.4 = (f32[7,16,75]{2,1,0:T(8,128)}, f32[7,16,75]{2,1,0:T(8,128)}, u32[]{:S(2)}, u32[]{:S(2)}) collective-permute-start(f32[7,16,75]{2,1,0:T(8,128)} %collective-permute-done.3), channel_id=1, source_target_pairs={{0,4},{4,0},{1,5},{5,1},{2,6},{6,2},{3,7},{7,3},{8,12},{12,8},{9,1... | collective-permute-start | bytes 100808 | tf_op jit(solution)/shard_map/ppermute | solution.py:29
  68.0 7.6 %scatter_custom_fusion = f32[4,1024]{0,1:T(8,128)} fusion(s32[1024]{0:T(1024)} %bitcast.2282, f32[1024]{0:T(1024)} %param.23, f32[]{:T(128)} %constant.17.clone.1, f32[]{:T(128)} %constant.9.clone.1, pred[1024]{0:T(1024)(128)(4,1)} %compare_and_fusion, f32[4,256]{0,1:T(8,128)S(1)} %copy.27992, s32[1024]{0:T(1024)} %fusion.221), kind=kCustom, calls=%fused_computation.31 | custom fusion | flops 8192 | bytes 30720 | tf_op jit(solution)/shard_map/scatter | solution.py:143
  77.6 4.7 %all-to-all-start.1 = ((f32[16,1,256]{2,1,0:T(1,128)}), f32[16,1,256]{2,1,0:T(1,128)S(1)}, u32[]{:S(2)}, u32[]{:S(2)}) async-start(f32[16,1,256]{2,1,0:T(1,128)} %reshape.23109), calls=%async_computation.1 | async-start | bytes 32768 | tf_op jit(solution)/shard_map/all_to_all | solution.py:146
  84.2 2.8 %collective-permute-start.5 = (f32[7,16,75]{2,1,0:T(8,128)}, f32[7,16,75]{2,1,0:T(8,128)}, u32[]{:S(2)}, u32[]{:S(2)}) collective-permute-start(f32[7,16,75]{2,1,0:T(8,128)} %collective-permute-done.4), channel_id=1, source_target_pairs={{0,8},{8,0},{1,9},{9,1},{2,10},{10,2},{3,11},{11,3},{4,12},{12,4},... | collective-permute-start | bytes 100808 | tf_op jit(solution)/shard_map/ppermute | solution.py:29
  87.1 1.7 %all-to-all-done.1 = f32[16,1,256]{2,1,0:T(1,128)S(1)} async-done(((f32[16,1,256]{2,1,0:T(1,128)}), f32[16,1,256]{2,1,0:T(1,128)S(1)}, u32[]{:S(2)}, u32[]{:S(2)}) %all-to-all-start.1) | async-done | bytes 16416 | tf_op jit(solution)/shard_map/all_to_all | solution.py:146
  91.1 7.4 %scatter_custom_fusion.1 = f32[4,2048]{0,1:T(8,128)} fusion(s32[1024]{0:T(1024)S(1)} %bitcast.2285, f32[1024,4]{1,0:T(8,128)} %bitcast.2272, f32[]{:T(128)} %constant.9.clone.1), kind=kCustom, calls=%fused_computation.34 | custom fusion | flops 4096 | bytes 33280 | tf_op jit(solution)/shard_map/scatter-add | solution.py:152
  98.5 1.6 %copy.28514 = f32[4,16,1,128]{3,1,0,2:T(8,128)S(1)} copy(f32[4,16,1,128]{0,3,1,2:T(8,128)} %bitcast.2269) | data formatting | bytes 65536 | tf_op jit(solution)/shard_map/reshape | solution.py:154
  100.1 1.6 %copy.27995 = f32[4,16,128]{2,1,0:T(8,128)S(1)} copy(f32[4,16,128]{0,2,1:T(8,128)} %bitcast.2270) | data formatting | bytes 65536 | tf_op jit(solution)/shard_map/reshape | solution.py:154
  105.2 3.3 %copy.27988 = f32[4,16,75,1]{3,1,0,2:T(8,128)} copy(f32[4,16,75,1]{2,1,0,3:T(8,128)S(1)} %multiply_bitcast_fusion) | data formatting | bytes 38400 | tf_op jit(solution)/shard_map/broadcast_in_dim | solution.py:132
  108.6 2.8 %maximum_bitcast_fusion = (f32[17,75,128]{2,0,1:T(8,128)S(1)}, f32[1,17,75,128]{3,1,0,2:T(8,128)S(1)}, f32[17,75,128]{2,0,1:T(8,128)}) fusion(f32[1,16,75,128]{3,1,0,2:T(8,128)} %copy-done.4, f32[1,16,75,128]{3,1,0,2:T(8,128)S(1)} %bitcast.2262, f32[1,16,75,128]{3,1,0,2:T(8,128)} %bitcast.2266, f32[7,1,75,128]{3,1,0,2:T(1,128)S(1)} %collective-permute-done, ...), kind=kLoop, calls=%fused_computation.19 | loop fusion | flops 2284800 | bytes 6796800 | tf_op jit(solution)/shard_map/mul | solution.py:34
  111.4 3.3 %maximum_maximum_fusion = (f32[7,17,75,128]{3,1,0,2:T(8,128)S(1)}, f32[7,17,75,128]{3,1,0,2:T(8,128)S(1)}) fusion(f32[1,16,75,128]{3,1,0,2:T(8,128)S(1)} %copy-done.5, f32[1,16,75,128]{3,1,0,2:T(8,128)S(1)} %bitcast.2263, f32[1,16,75,128]{3,1,0,2:T(8,128)S(1)} %bitcast.2267, f32[7,1,75,128]{3,1,0,2:T(1,128)S(1)} %collective-permute-done, ...), kind=kLoop, calls=%fused_computation.4 | loop fusion | flops 9139200 | bytes 13977600 | tf_op jit(solution)/shard_map/concatenate | solution.py:90
  114.7 2.2 %fusion.3 = (f32[17,75,128]{2,0,1:T(8,128)}, f32[17,75,128]{2,0,1:T(8,128)}) fusion(f32[7,1,75,128]{3,1,0,2:T(1,128)} %collective-permute-done.1, f32[1,16,75,128]{3,1,0,2:T(8,128)S(1)} %copy-done.5, f32[1,16,75,128]{3,1,0,2:T(8,128)S(1)} %bitcast.2264, f32[1,16,75,128]{3,1,0,2:T(8,128)S(1)} %bitcast.2268, f32[7,1,75,128]{3,1,0,2:T(1,128)S(1)} %collective-permute-done, ...), kind=kLoop, calls=%fused_computation.14 | loop fusion | flops 1795200 | bytes 6796800 | tf_op jit(solution)/shard_map/mul | solution.py:36
  116.9 3.5 %add_multiply_fusion = f32[4,17,75,128]{3,1,0,2:T(8,128)S(1)} fusion(f32[7,17,75,128]{3,1,0,2:T(8,128)S(1)} %get-tuple-element.196, f32[7,17,75,128]{3,1,0,2:T(8,128)S(1)} %get-tuple-element.195, f32[17,75,128]{2,0,1:T(8,128)} %get-tuple-element.401, f32[17,75,128]{2,0,1:T(8,128)} %get-tuple-element.402, f32[17,75,128]{2,0,1:T(8,128)S(1)} %get-tuple-element.192, ...), kind=kLoop, calls=%fused_computation.6 | loop fusion | flops 4569600 | bytes 10444800 | tf_op jit(solution)/shard_map/mul | solution.py:33
  120.9 3.2 %fusion.1 = f32[4,16,75,128]{3,1,0,2:T(8,128)S(1)} fusion(f32[4,17,75,128]{3,1,0,2:T(8,128)S(1)} %add_multiply_fusion, f32[4,16,75,1]{3,1,0,2:T(8,128)} %copy.27988, f32[4,16,75,127]{3,1,0,2:T(8,128)S(1)} %copy-done.7, f32[4,16,75,128]{3,1,2,0:T(8,128)S(1)} %copy-done), kind=kLoop, calls=%fused_computation.9 | loop fusion | flops 3072000 | bytes 12288000 | tf_op jit(solution)/shard_map/sub | solution.py:134
  125.7 3.0 %fusion.41 = (f32[4,16,128]{2,1,0:T(8,128)S(1)}, f32[4,16,128]{2,1,0:T(8,128)S(1)}, f32[4,16,128]{2,1,0:T(8,128)S(1)}, f32[4,16,128]{2,1,0:T(8,128)S(1)}, f32[4,...) fusion(f32[4,16,75,128]{3,1,0,2:T(8,128)S(1)} %fusion.1, ...), kind=kLoop, calls=%fused_computation.156 | loop fusion | flops 2162688 | bytes 4669440 | tf_op jit(solution)/shard_map/div | solution.py:57
  129.1 2.8 %constant_dynamic-update-slice_fusion.74 = (f32[4,16,75,128]{3,1,0,2:T(8,128)S(1)}, f32[4,16,128]{2,1,0:T(8,128)S(1)}, f32[4,16,128]{2,1,0:T(8,128)S(1)}, f32[4,...) fusion(f32[16,128]{1,0:T(8,128)} %get-tuple-element.191, ...), kind=kLoop, calls=%fused_computation.118 | loop fusion | flops 2818047 | bytes 5185536
  135.8 3.5 %constant_dynamic-update-slice_fusion.62 = (f32[4,16,75,128]{3,1,0,2:T(8,128)S(1)}, f32[4,16,1,128]{3,1,0,2:T(8,128)S(1)}, f32[4,16,1,128]{3,1,0,2:T(8,128)S(1)}...) fusion(f32[4,16,75,128]{3,1,0,2:T(8,128)S(1)} %constant_dynamic, ...), kind=kLoop, calls=%fused_computation.106 | loop fusion | flops 3014656 | bytes 5021696
  140.4 1.6 %copy.28611 = f32[4,16,75,128]{3,1,2,0:T(8,128)} copy(f32[4,16,75,128]{3,1,0,2:T(8,128)S(1)} %constant_dynamic-update-slice_fusion) | data formatting | bytes 4915200 | tf_op jit(solution)/shard_map/stack | solution.py:65
  (459 shorter events, 41.5 us)
Async XLA Ops:
  4.2 104.4 %collective-permute-start = (f32[7,1,75,128]{3,1,0,2:T(1,128)}, f32[7,1,75,128]{3,1,0,2:T(1,128)S(1)}, u32[]{:S(2)}, u32[]{:S(2)}) collective-permute-start(f32[7,1,75,128]{3,1,0,2:T(1,128)} %get-tuple-element.197), channel_id=1, source_target_pairs={{0,1},{1,2},{2,3},{3,4},{4,5},{5,6},{6,7},{7,8},{8,9},{9,10},{10,1... | collective-permute-start | bytes 806408 | tf_op jit(solution)/shard_map/ppermute | solution.py:16
  4.6 103.9 %collective-permute-start.1 = (f32[7,1,75,128]{3,1,0,2:T(1,128)}, f32[7,1,75,128]{3,1,0,2:T(1,128)}, u32[]{:S(2)}, u32[]{:S(2)}) collective-permute-start(f32[7,1,75,128]{3,1,0,2:T(1,128)} %get-tuple-element.198), channel_id=1, source_target_pairs={{1,0},{2,1},{3,2},{4,3},{5,4},{6,5},{7,6},{8,7},{9,8},{10,9},{11,1... | collective-permute-start | bytes 806408 | tf_op jit(solution)/shard_map/ppermute | solution.py:17
  15.3 13.2 %copy-start.152 = (s32[2]{0:T(128)S(1)}, s32[2]{0:T(128)}, u32[]{:S(2)}) copy-start(s32[2]{0:T(128)} %constant.24) | copy-start | bytes 28
  15.3 13.3 %copy-start.153 = (s32[2]{0:T(128)S(1)}, s32[2]{0:T(128)}, u32[]{:S(2)}) copy-start(s32[2]{0:T(128)} %constant.53) | copy-start | bytes 28
  23.5 36.9 %collective-permute-start.2 = (f32[7,16,75]{2,1,0:T(8,128)}, f32[7,16,75]{2,1,0:T(8,128)}, u32[]{:S(2)}, u32[]{:S(2)}) collective-permute-start(f32[7,16,75]{2,1,0:T(8,128)} %pad_maximum_fusion.6), channel_id=1, source_target_pairs={{0,1},{1,0},{2,3},{3,2},{4,5},{5,4},{6,7},{7,6},{8,9},{9,8},{10,11... | collective-permute-start | bytes 100808 | tf_op jit(solution)/shard_map/ppermute | solution.py:29
  28.6 11.7 %copy-start.149 = (s32[1024,1]{0,1:T(1,128)}, s32[1024,1]{0,1:T(1,128)S(1)}, u32[]{:S(2)}) copy-start(s32[1024,1]{0,1:T(1,128)S(1)} %compare_select_fusion.1) | copy-start | bytes 12292
  33.9 43.7 %all-to-all-start = ((s32[1,16,64]{2,0,1:T(1,128)}), s32[1,16,64]{2,0,1:T(1,128)}, u32[]{:S(2)}, u32[]{:S(2)}) async-start(s32[1,16,64]{2,0,1:T(1,128)} %bitcast.23), calls=%async_computation | async-start | bytes 16384 | tf_op jit(solution)/shard_map/all_to_all | solution.py:147
  42.7 13.7 %copy-start.34 = (f32[16,128]{1,0:T(8,128)}, f32[16,128]{1,0:T(8,128)S(1)}, u32[]{:S(2)}) copy-start(f32[16,128]{1,0:T(8,128)S(1)} %get-tuple-element.153) | copy-start | bytes 24580
  42.7 13.7 %copy-start.131 = (f32[16,128]{1,0:T(8,128)}, f32[16,128]{1,0:T(8,128)S(1)}, u32[]{:S(2)}) copy-start(f32[16,128]{1,0:T(8,128)S(1)} %get-tuple-element.181) | copy-start | bytes 24580
  42.8 13.7 %copy-start.132 = (f32[16,128]{1,0:T(8,128)}, f32[16,128]{1,0:T(8,128)S(1)}, u32[]{:S(2)}) copy-start(f32[16,128]{1,0:T(8,128)S(1)} %get-tuple-element.183) | copy-start | bytes 24580
  42.8 13.7 %copy-start.133 = (f32[16,128]{1,0:T(8,128)}, f32[16,128]{1,0:T(8,128)S(1)}, u32[]{:S(2)}) copy-start(f32[16,128]{1,0:T(8,128)S(1)} %get-tuple-element.185) | copy-start | bytes 24580
  42.8 13.7 %copy-start.134 = (f32[16,128]{1,0:T(8,128)}, f32[16,128]{1,0:T(8,128)S(1)}, u32[]{:S(2)}) copy-start(f32[16,128]{1,0:T(8,128)S(1)} %get-tuple-element.187) | copy-start | bytes 24580
  42.8 13.7 %copy-start.135 = (f32[16,128]{1,0:T(8,128)}, f32[16,128]{1,0:T(8,128)S(1)}, u32[]{:S(2)}) copy-start(f32[16,128]{1,0:T(8,128)S(1)} %get-tuple-element.189) | copy-start | bytes 24580
  42.8 13.7 %copy-start.136 = (f32[16,128]{1,0:T(8,128)}, f32[16,128]{1,0:T(8,128)S(1)}, u32[]{:S(2)}) copy-start(f32[16,128]{1,0:T(8,128)S(1)} %get-tuple-element.180) | copy-start | bytes 24580
  42.8 13.7 %copy-start.137 = (f32[16,128]{1,0:T(8,128)}, f32[16,128]{1,0:T(8,128)S(1)}, u32[]{:S(2)}) copy-start(f32[16,128]{1,0:T(8,128)S(1)} %get-tuple-element.182) | copy-start | bytes 24580
  42.8 13.7 %copy-start.138 = (f32[16,128]{1,0:T(8,128)}, f32[16,128]{1,0:T(8,128)S(1)}, u32[]{:S(2)}) copy-start(f32[16,128]{1,0:T(8,128)S(1)} %get-tuple-element.184) | copy-start | bytes 24580
  42.8 13.7 %copy-start.139 = (f32[16,128]{1,0:T(8,128)}, f32[16,128]{1,0:T(8,128)S(1)}, u32[]{:S(2)}) copy-start(f32[16,128]{1,0:T(8,128)S(1)} %get-tuple-element.186) | copy-start | bytes 24580
  42.8 13.7 %copy-start.140 = (f32[16,128]{1,0:T(8,128)}, f32[16,128]{1,0:T(8,128)S(1)}, u32[]{:S(2)}) copy-start(f32[16,128]{1,0:T(8,128)S(1)} %get-tuple-element.188) | copy-start | bytes 24580
  42.8 13.7 %copy-start.141 = (f32[16,128]{1,0:T(8,128)}, f32[16,128]{1,0:T(8,128)S(1)}, u32[]{:S(2)}) copy-start(f32[16,128]{1,0:T(8,128)S(1)} %get-tuple-element.190) | copy-start | bytes 24580
  49.2 9.4 %copy-start.21 = (f32[16,128]{1,0:T(8,128)}, f32[16,128]{1,0:T(8,128)S(1)}, u32[]{:S(2)}) copy-start(f32[16,128]{1,0:T(8,128)S(1)} %get-tuple-element.88) | copy-start | bytes 24580
  49.2 9.4 %copy-start.93 = (f32[16,128]{1,0:T(8,128)}, f32[16,128]{1,0:T(8,128)S(1)}, u32[]{:S(2)}) copy-start(f32[16,128]{1,0:T(8,128)S(1)} %get-tuple-element.75) | copy-start | bytes 24580
  49.2 10.0 %copy-start.23 = (f32[16,128]{1,0:T(8,128)}, f32[16,128]{1,0:T(8,128)S(1)}, u32[]{:S(2)}) copy-start(f32[16,128]{1,0:T(8,128)S(1)} %get-tuple-element.90) | copy-start | bytes 24580
  49.2 10.0 %copy-start.94 = (f32[16,128]{1,0:T(8,128)}, f32[16,128]{1,0:T(8,128)S(1)}, u32[]{:S(2)}) copy-start(f32[16,128]{1,0:T(8,128)S(1)} %get-tuple-element.77) | copy-start | bytes 24580
  49.2 10.0 %copy-start.100 = (f32[16,128]{1,0:T(8,128)}, f32[16,128]{1,0:T(8,128)S(1)}, u32[]{:S(2)}) copy-start(f32[16,128]{1,0:T(8,128)S(1)} %get-tuple-element.89) | copy-start | bytes 24580
  49.3 10.6 %copy-start.11 = (f32[16,128]{1,0:T(8,128)}, f32[16,128]{1,0:T(8,128)S(1)}, u32[]{:S(2)}) copy-start(f32[16,128]{1,0:T(8,128)S(1)} %get-tuple-element.78) | copy-start | bytes 24580
  60.5 4.6 %collective-permute-start.3 = (f32[7,16,75]{2,1,0:T(8,128)}, f32[7,16,75]{2,1,0:T(8,128)}, u32[]{:S(2)}, u32[]{:S(2)}) collective-permute-start(f32[7,16,75]{2,1,0:T(8,128)} %collective-permute-done.2), channel_id=1, source_target_pairs={{0,2},{2,0},{1,3},{3,1},{4,6},{6,4},{5,7},{7,5},{8,10},{10,8},{9,1... | collective-permute-start | bytes 100808 | tf_op jit(solution)/shard_map/ppermute | solution.py:29
  65.1 19.2 %collective-permute-start.4 = (f32[7,16,75]{2,1,0:T(8,128)}, f32[7,16,75]{2,1,0:T(8,128)}, u32[]{:S(2)}, u32[]{:S(2)}) collective-permute-start(f32[7,16,75]{2,1,0:T(8,128)} %collective-permute-done.3), channel_id=1, source_target_pairs={{0,4},{4,0},{1,5},{5,1},{2,6},{6,2},{3,7},{7,3},{8,12},{12,8},{9,1... | collective-permute-start | bytes 100808 | tf_op jit(solution)/shard_map/ppermute | solution.py:29
  75.6 26.9 %copy-start.145 = (f32[16,75,1]{1,0,2:T(8,128)S(1)}, f32[16,75,1]{1,0,2:T(8,128)}, u32[]{:S(2)}) copy-start(f32[16,75,1]{1,0,2:T(8,128)} %copy-done.144) | copy-start | bytes 14404
  75.6 26.9 %copy-start.147 = (f32[16,75,1]{1,0,2:T(8,128)S(1)}, f32[16,75,1]{1,0,2:T(8,128)}, u32[]{:S(2)}) copy-start(f32[16,75,1]{1,0,2:T(8,128)} %copy-done.146) | copy-start | bytes 14404
  75.6 27.5 %copy-start.143 = (f32[16,75,1]{1,0,2:T(8,128)S(1)}, f32[16,75,1]{1,0,2:T(8,128)}, u32[]{:S(2)}) copy-start(f32[16,75,1]{1,0,2:T(8,128)} %copy-done.142) | copy-start | bytes 14404
  77.6 11.2 %all-to-all-start.1 = ((f32[16,1,256]{2,1,0:T(1,128)}), f32[16,1,256]{2,1,0:T(1,128)S(1)}, u32[]{:S(2)}, u32[]{:S(2)}) async-start(f32[16,1,256]{2,1,0:T(1,128)} %reshape.23109), calls=%async_computation.1 | async-start | bytes 32768 | tf_op jit(solution)/shard_map/all_to_all | solution.py:146
  84.2 17.4 %collective-permute-start.5 = (f32[7,16,75]{2,1,0:T(8,128)}, f32[7,16,75]{2,1,0:T(8,128)}, u32[]{:S(2)}, u32[]{:S(2)}) collective-permute-start(f32[7,16,75]{2,1,0:T(8,128)} %collective-permute-done.4), channel_id=1, source_target_pairs={{0,8},{8,0},{1,9},{9,1},{2,10},{10,2},{3,11},{11,3},{4,12},{12,4},... | collective-permute-start | bytes 100808 | tf_op jit(solution)/shard_map/ppermute | solution.py:29
  (132 other events, 670.1 us)
where the time goes:
time: 144 us; the launch traced here: 142 us
  other arithmetic  72.8 us (51%)
  local copies, waits for them, and re-layouts  42 us (29%)
  starting transfers between devices  20.3 us (14%)
  waiting for transfers between devices  4.13 us (3%)
  between operations  2.83 us (2%)
    unnamed x40, other arithmetic  10.3 us
    sub x13, other arithmetic, mix_columns(): here_thickness + here_coupling + prior_coupling  9.39 us
    unnamed x349, local copies, waits for them, and re-layouts  7.9 us
    scatter x1, other arithmetic, shards(): jnp.zeros((tracer_count, cycle_size * CAP), jnp.float32).at[:, position]  7.59 us
    scatter-add x1, other arithmetic, shards(): surface = jnp.zeros((tracer_count, lon_cells * lat_cells), jnp.float32).a...  7.4 us
    mul x3, other arithmetic, face_flux(): open_face * (jnp.maximum(speed, 0.0) * near + jnp.minimum(speed, 0.0) * f...  6.84 us
    ppermute x4, starting transfers between devices, from_partner(): return lax.ppermute(block, axis, route)  5.91 us
    ppermute x1, starting transfers between devices, padded_2(): after = lax.ppermute(leading, axis, down)  4.99 us
  transfers between devices with their start and end apart: 8, of which 2 were waited for; matrix products, arithmetic and copies ran while one was open for 54% of the time, Pallas kernels for 0%

commit v1 on v0

v1 whole, which is shorter than its diff:
```python
import functools

import jax
import jax.numpy as jnp
from jax import lax
from jax.experimental import pallas as pl
from jax.experimental.pallas import tpu as pltpu
from jax.sharding import PartitionSpec as P

CAP = 64
HALF = 8
LANES = 128
F32 = jnp.float32


def chunk_of(levels):
    return max(c for c in range(1, 16) if levels % c == 0)


def thirds(x):
    high = x.astype(jnp.bfloat16)
    rest = x - high.astype(F32)
    mid = rest.astype(jnp.bfloat16)
    low = (rest - mid.astype(F32)).astype(jnp.bfloat16)
    return high, mid, low


def lane_ids(rows):
    return lax.broadcasted_iota(jnp.int32, (rows, LANES), 1)


def row_ids(rows):
    return lax.broadcasted_iota(jnp.int32, (rows, LANES), 0)


def dot_nt(a, b):
    return lax.dot_general(a, b, (((1,), (1,)), ((), ())), preferred_element_type=F32)


def dot_nn(a, b):
    return lax.dot_general(a, b, (((1,), (0,)), ((), ())), preferred_element_type=F32)


def make_messages(tiles, air_ref, tile_ref, source_ref, cell_ref, weight_ref, msg_ref):
    count, air_cells = air_ref.shape
    chunks = tile_ref.shape[0]
    one, zero = jnp.ones((), F32), jnp.zeros((), F32)
    rows = [slice(c, c + 1) for c in range(chunks)]
    owns = [
        jnp.broadcast_to(tile_ref[r, :], (tiles, LANES)) == row_ids(tiles) for r in rows
    ]
    owned = jnp.concatenate([jnp.where(o, one, zero) for o in owns], axis=0).astype(jnp.bfloat16)
    earlier = jnp.where(row_ids(LANES) < lane_ids(LANES), one, zero).astype(jnp.bfloat16)
    prior = dot_nn(owned, earlier)
    total = dot_nn(owned, jnp.ones((LANES, LANES), jnp.bfloat16))
    air_parts = jnp.concatenate(
        [p.astype(F32) for p in thirds(air_ref[...])], axis=0
    ).astype(jnp.bfloat16)
    carry = jnp.zeros((tiles, LANES), F32)
    slots, parts = [], []
    for c in range(chunks):
        span = slice(c * tiles, (c + 1) * tiles)
        slots.append(
            jnp.sum(jnp.where(owns[c], prior[span] + carry, zero), axis=0, keepdims=True)
        )
        carry = carry + total[span]
        picked = jnp.broadcast_to(source_ref[rows[c], :], (air_cells, LANES)) == row_ids(air_cells)
        taken = dot_nn(air_parts, jnp.where(picked, one, zero).astype(jnp.bfloat16))
        flux = taken[:count] + taken[count : 2 * count] + taken[2 * count : 3 * count]
        payload = weight_ref[rows[c], :] * flux
        record = jnp.concatenate(
            [
                payload,
                cell_ref[rows[c], :].astype(F32),
                jnp.zeros((HALF - count - 1, LANES), F32),
            ],
            axis=0,
        )
        parts.append([p.astype(F32) for p in thirds(record)])
    slot_hot = jnp.concatenate(
        [
            jnp.where(
                jnp.broadcast_to(s.astype(jnp.int32), (LANES, LANES)) == row_ids(LANES), one, zero
            ).astype(jnp.bfloat16)
            for s in slots
        ],
        axis=1,
    )
    out = jnp.zeros((tiles * HALF, LANES), F32)
    for part in range(3):
        spread = jnp.concatenate(
            [
                jnp.concatenate(
                    [
                        jnp.where(
                            jnp.broadcast_to(tile_ref[rows[c], :], (HALF, LANES)) == d,
                            parts[c][part],
                            zero,
                        )
                        for d in range(tiles)
                    ],
                    axis=0,
                ).astype(jnp.bfloat16)
                for c in range(chunks)
            ],
            axis=1,
        )
        out = out + dot_nt(spread, slot_hot)
    msg_ref[...] = out.reshape(tiles, HALF, LANES)


def pack_kernel(
    levels,
    tiles,
    tracer_ref,
    east_ref,
    north_ref,
    kappa_ref,
    depth_ref,
    air_ref,
    tile_ref,
    source_ref,
    cell_ref,
    weight_ref,
    up_ref,
    down_ref,
    mirror_ref,
    msg_ref,
    column_ref,
):
    step = pl.program_id(0)
    count, chunk, cells, _ = tracer_ref.shape
    fields = count + 2
    lane = lane_ids(cells)

    @pl.when(step == 0)
    def _():
        depth = depth_ref[...].astype(F32)
        up_ref[fields * levels : fields * levels + 1, :] = depth[cells - 1 : cells]
        down_ref[(fields - 1) * levels : (fields - 1) * levels + 1, :] = depth[0:1]
        column_ref[...] = jnp.zeros_like(column_ref)
        column_ref[0] = jnp.where(lane == levels, pltpu.roll(depth, levels + 1, 1), 0.0)
        make_messages(tiles, air_ref, tile_ref, source_ref, cell_ref, weight_ref, msg_ref)

    columns = [column_ref[f] for f in range(fields)]
    for here in range(chunk):
        k = step * chunk + here
        slabs = [tracer_ref[n, here] for n in range(count)] + [north_ref[here], kappa_ref[here]]
        for f in range(fields):
            columns[f] = jnp.where(lane == k, pltpu.roll(slabs[f], k + 1, 1), columns[f])
            if f < count:
                up_ref[pl.ds(f * levels + k, 1), :] = slabs[f][cells - 1 : cells]
                down_ref[pl.ds(f * levels + k, 1), :] = slabs[f][0:1]
        up_ref[pl.ds(count * levels + k, 1), :] = east_ref[here][HALF - 1 : HALF]
        up_ref[pl.ds((count + 1) * levels + k, 1), :] = slabs[count + 1][cells - 1 : cells]
        down_ref[pl.ds(count * levels + k, 1), :] = slabs[count + 1][0:1]
    for f in range(fields):
        column_ref[f] = columns[f]

    @pl.when(step == pl.num_programs(0) - 1)
    def _():
        for f in range(fields):
            for i in range(cells):
                mirror_ref[f * cells + cells - 1 - i : f * cells + cells - i, :] = columns[f][
                    i : i + 1
                ]


def pack(tiles, tracer, east, north, kappa, depth, air, tile, source, cell, weight):
    count, levels, cells, lat = tracer.shape
    fields = count + 2
    chunk = chunk_of(levels)
    whole = lambda x: pl.BlockSpec(x.shape, lambda s, nd=x.ndim: (0,) * nd)
    level = lambda s: (s, 0, 0)
    out = [
        jax.ShapeDtypeStruct((-(-(fields * levels + 1) // HALF) * HALF, lat), F32),
        jax.ShapeDtypeStruct((-(-((fields - 1) * levels + 1) // HALF) * HALF, lat), F32),
        jax.ShapeDtypeStruct((fields * cells, LANES), F32),
        jax.ShapeDtypeStruct((tiles, HALF, LANES), F32),
    ]
    return pl.pallas_call(
        functools.partial(pack_kernel, levels, tiles),
        grid=(levels // chunk,),
        out_shape=out,
        in_specs=[
            pl.BlockSpec((count, chunk, cells, lat), lambda s: (0, s, 0, 0)),
            pl.BlockSpec((chunk, HALF, lat), lambda s: (s, cells // HALF - 1, 0)),
            pl.BlockSpec((chunk, cells, lat), level),
            pl.BlockSpec((chunk, cells, lat), level),
        ]
        + [whole(x) for x in (depth, air, tile, source, cell, weight)],
        out_specs=[whole(o) for o in out],
        scratch_shapes=[pltpu.VMEM((fields, cells, LANES), F32)],
        compiler_params=pltpu.CompilerParams(vmem_limit_bytes=24 << 20),
        cost_estimate=pl.CostEstimate(flops=10**7, bytes_accessed=4 * 10**6, transcendentals=0),
        name="pack",
    )(tracer, east, north, kappa, depth, air, tile, source, cell, weight)


def gather_surface(count, cells, lat, received_ref):
    tiles = received_ref.shape[0]
    shift = lat.bit_length() - 1
    values, spots = [[], [], []], []
    one, zero = jnp.ones((), F32), jnp.zeros((), F32)
    left, right = [[], [], []], []
    for t in range(tiles):
        block = received_ref[t]
        cell = block[count : count + 1].astype(jnp.int32)
        row = jnp.broadcast_to(lax.shift_right_logical(cell, shift), (cells, LANES))
        col = jnp.broadcast_to(cell & (lat - 1), (lat, LANES))
        right.append(jnp.where(col == row_ids(lat), one, zero).astype(jnp.bfloat16))
        hit = row == row_ids(cells)
        for p, part in enumerate(thirds(block)):
            part = part.astype(F32)
            left[p].append(
                jnp.concatenate(
                    [
                        jnp.where(hit, jnp.broadcast_to(part[n : n + 1], (cells, LANES)), zero)
                        for n in range(count)
                    ],
                    axis=0,
                ).astype(jnp.bfloat16)
            )
    spread = jnp.concatenate(right, axis=1)
    return sum(dot_nt(jnp.concatenate(left[p], axis=1), spread) for p in range(3))


def step_kernel(
    levels,
    tracer_ref,
    east_ref,
    north_ref,
    kappa_ref,
    mixing_ref,
    thick_ref,
    depth_ref,
    west_ref,
    far_ref,
    mirror_ref,
    received_ref,
    out_ref,
    value_ref,
    gain_ref,
    rhs_ref,
    thickness_ref,
    coupling_ref,
    limit_ref,
):
    step = pl.program_id(0)
    count, chunk, cells, lat = tracer_ref.shape
    blocks = pl.num_programs(0) // 2
    halves = cells // HALF
    fields = count + 2
    row8 = row_ids(HALF)
    lane8 = lane_ids(HALF)
    top = lane8 == lat - 1
    bottom = lane8 == 0
    first = row8 == 0
    last = row8 == HALF - 1
    hs = [slice(h * HALF, (h + 1) * HALF) for h in range(halves)]

    def from_east(parts, halo):
        turned = [pltpu.roll(p, HALF - 1, 0) for p in parts]
        return [
            jnp.where(last, turned[h + 1] if h + 1 < halves else halo, turned[h])
            for h in range(halves)
        ]

    def from_west(parts, halo):
        turned = [pltpu.roll(p, 1, 0) for p in parts]
        return [
            jnp.where(first, turned[h - 1] if h > 0 else halo, turned[h]) for h in range(halves)
        ]

    def row_of(ref, index):
        return jnp.broadcast_to(ref[pl.ds(index, 1), :], (HALF, lat))

    def mirrored(field, h, k):
        spot = field * cells + h * HALF
        return pltpu.roll(mirror_ref[spot : spot + HALF, :], lat - 1 - k, 1)

    @pl.when(step == 0)
    def _():
        depth = [depth_ref[s, :].astype(F32) for s in hs]
        east = from_east(depth, row_of(far_ref, (fields - 1) * levels))
        for h in range(halves):
            limit_ref[0, hs[h], :] = jnp.minimum(depth[h], east[h])
            north = jnp.where(top, mirrored(0, h, levels), pltpu.roll(depth[h], lat - 1, 1))
            limit_ref[1, hs[h], :] = jnp.minimum(depth[h], north)
            limit_ref[2, hs[h], :] = depth[h]
        limit_ref[3, 0:HALF, :] = jnp.minimum(
            jnp.broadcast_to(depth[0][0:1], (HALF, lat)), row_of(west_ref, fields * levels)
        )
        rhs_ref[...] = jnp.zeros_like(rhs_ref)
        thickness_ref[...] = jnp.ones_like(thickness_ref)
        coupling_ref[...] = jnp.zeros_like(coupling_ref)
        value_ref[:, levels] = jnp.zeros((count, cells, lat), F32)
        gain_ref[levels] = jnp.zeros((cells, lat), F32)

    @pl.when(step < blocks)
    def _():
        block = blocks - 1 - step
        limit_east = [limit_ref[0, s, :] for s in hs]
        limit_north = [limit_ref[1, s, :] for s in hs]
        limit_here = [limit_ref[2, s, :] for s in hs]
        limit_west = limit_ref[3, 0:HALF, :]
        rhs = [[rhs_ref[n, s, :] for s in hs] for n in range(count)]
        thick_below = [thickness_ref[s, :] for s in hs]
        coupling_below = [coupling_ref[s, :] for s in hs]
        held = block * chunk + chunk
        value = [[value_ref[n, jnp.minimum(held + 1, levels), s, :] for s in hs] for n in range(count)]
        gain = [gain_ref[jnp.minimum(held + 1, levels), s, :] for s in hs]
        for here in range(chunk - 1, -1, -1):
            k = block * chunk + here
            level = k.astype(F32)
            kappa = [kappa_ref[here, s, :] for s in hs]
            speed = [east_ref[here, s, :] for s in hs]
            kappa_east = from_east(kappa, row_of(far_ref, count * levels + k))
            near_e, far_e = [], []
            for h in range(halves):
                mean = 0.5 * (kappa[h] + kappa_east[h])
                open_face = limit_east[h] > level
                near_e.append(jnp.where(open_face, jnp.maximum(speed[h], 0.0) + mean, 0.0))
                far_e.append(jnp.where(open_face, jnp.minimum(speed[h], 0.0) - mean, 0.0))
            speed_w = row_of(west_ref, count * levels + k)
            mean = 0.5 * (row_of(west_ref, (count + 1) * levels + k) + jnp.broadcast_to(kappa[0][0:1], (HALF, lat)))
            open_face = limit_west > level
            near_w = jnp.where(open_face, jnp.maximum(speed_w, 0.0) + mean, 0.0)
            far_w = jnp.where(open_face, jnp.minimum(speed_w, 0.0) - mean, 0.0)
            near_n, far_n = [], []
            for h in range(halves):
                speed_n = north_ref[here, hs[h], :]
                speed_n = jnp.where(top, 0.5 * (speed_n - mirrored(count, h, k)), speed_n)
                kappa_n = jnp.where(
                    top, mirrored(count + 1, h, k), pltpu.roll(kappa[h], lat - 1, 1)
                )
                mean = 0.5 * (kappa[h] + kappa_n)
                open_face = limit_north[h] > level
                near_n.append(jnp.where(open_face, jnp.maximum(speed_n, 0.0) + mean, 0.0))
                far_n.append(jnp.where(open_face, jnp.minimum(speed_n, 0.0) - mean, 0.0))
            thick = [thick_ref[here, s, :] for s in hs]
            coupling, scale = [], []
            for h in range(halves):
                wet_below = limit_here[h] > level + 1.0
                here_c = jnp.where(
                    wet_below,
                    2.0 * mixing_ref[here, hs[h], :] / (thick[h] + thick_below[h]),
                    0.0,
                )
                coupling.append(here_c)
                pivot = thick_below[h] + here_c + coupling_below[h] - coupling_below[h] * gain[h]
                scale.append(1.0 / pivot)
            for h in range(halves):
                gain[h] = coupling[h] * scale[h]
                gain_ref[k + 1, hs[h], :] = gain[h]
            for n in range(count):
                cell = [tracer_ref[n, here, s, :] for s in hs]
                cell_east = from_east(cell, row_of(far_ref, n * levels + k))
                flux_e = [near_e[h] * cell[h] + far_e[h] * cell_east[h] for h in range(halves)]
                flux_in = near_w * row_of(west_ref, n * levels + k) + far_w * jnp.broadcast_to(
                    cell[0][0:1], (HALF, lat)
                )
                flux_w = from_west(flux_e, flux_in)
                for h in range(halves):
                    cell_north = jnp.where(
                        top, mirrored(n, h, k), pltpu.roll(cell[h], lat - 1, 1)
                    )
                    flux_n = near_n[h] * cell[h] + far_n[h] * cell_north
                    flux_s = jnp.where(bottom, 0.0, pltpu.roll(flux_n, 1, 1))
                    stepped = (cell[h] - (flux_e[h] - flux_w[h])) - (flux_n - flux_s)
                    value[n][h] = (rhs[n][h] + coupling_below[h] * value[n][h]) * scale[h]
                    value_ref[n, k + 1, hs[h], :] = value[n][h]
                    rhs[n][h] = thick[h] * stepped
            thick_below, coupling_below = thick, coupling
        for h in range(halves):
            for n in range(count):
                rhs_ref[n, hs[h], :] = rhs[n][h]
            thickness_ref[hs[h], :] = thick_below[h]
            coupling_ref[hs[h], :] = coupling_below[h]

    @pl.when(step == blocks)
    def _():
        surface = gather_surface(count, cells, lat, received_ref)
        for h in range(halves):
            coupling = coupling_ref[hs[h], :]
            pivot = thickness_ref[hs[h], :] + coupling - coupling * gain_ref[1, hs[h], :]
            scale = 1.0 / pivot
            wet = limit_ref[2, hs[h], :] > 0.0
            for n in range(count):
                spot = n * cells + h * HALF
                rhs = rhs_ref[n, hs[h], :] + jnp.where(wet, surface[spot : spot + HALF], 0.0)
                value_ref[n, 0, hs[h], :] = (rhs + coupling * value_ref[n, 1, hs[h], :]) * scale
        gain_ref[0] = jnp.zeros((cells, lat), F32)
        rhs_ref[...] = jnp.zeros_like(rhs_ref)

    @pl.when(step >= blocks)
    def _():
        block = step - blocks
        solved = [[rhs_ref[n, s, :] for s in hs] for n in range(count)]
        for here in range(chunk):
            k = block * chunk + here
            for h in range(halves):
                gain = gain_ref[k, hs[h], :]
                for n in range(count):
                    solved[n][h] = value_ref[n, k, hs[h], :] + gain * solved[n][h]
                    out_ref[n, here, hs[h], :] = solved[n][h]
        for h in range(halves):
            for n in range(count):
                rhs_ref[n, hs[h], :] = solved[n][h]


def step_columns(
    tracer, east, north, kappa, mixing, thickness, depth, west, far, mirror, received
):
    count, levels, cells, lat = tracer.shape
    chunk = chunk_of(levels)
    blocks = levels // chunk
    whole = lambda x: pl.BlockSpec(x.shape, lambda s, nd=x.ndim: (0,) * nd)
    read = lambda s: jnp.maximum(blocks - 1 - s, 0)
    write = lambda s: jnp.maximum(s - blocks, 0)
    level = pl.BlockSpec((chunk, cells, lat), lambda s: (read(s), 0, 0))
    return pl.pallas_call(
        functools.partial(step_kernel, levels),
        grid=(2 * blocks,),
        out_shape=jax.ShapeDtypeStruct(tracer.shape, F32),
        in_specs=[pl.BlockSpec((count, chunk, cells, lat), lambda s: (0, read(s), 0, 0))]
        + [level] * 5
        + [whole(x) for x in (depth, west, far, mirror, received)],
        out_specs=pl.BlockSpec((count, chunk, cells, lat), lambda s: (0, write(s), 0, 0)),
        scratch_shapes=[
            pltpu.VMEM((count, levels + 1, cells, lat), F32),
            pltpu.VMEM((levels + 1, cells, lat), F32),
            pltpu.VMEM((count, cells, lat), F32),
            pltpu.VMEM((cells, lat), F32),
            pltpu.VMEM((cells, lat), F32),
            pltpu.VMEM((4, cells, lat), F32),
        ],
        compiler_params=pltpu.CompilerParams(vmem_limit_bytes=40 << 20),
        cost_estimate=pl.CostEstimate(flops=10**8, bytes_accessed=8 * 10**6, transcendentals=0),
        name="columns",
    )(tracer, east, north, kappa, mixing, thickness, depth, west, far, mirror, received)


def shards(
    tracer,
    east_speed,
    north_speed,
    diffusivity,
    mixing,
    thickness,
    depth_levels,
    air_flux,
    margin_tile,
    margin_source,
    margin_cell,
    margin_weight,
):
    tiles = lax.axis_size("lon")
    by_level = lambda x: jnp.transpose(x, (1, 0, 2))
    tracer = jnp.transpose(tracer, (0, 2, 1, 3))
    east, north, kappa = by_level(east_speed), by_level(north_speed), by_level(diffusivity)
    rows = lambda x: x.reshape(-1, LANES)
    up, down, mirror, messages = pack(
        tiles,
        tracer,
        east,
        north,
        kappa,
        depth_levels,
        air_flux,
        rows(margin_tile),
        rows(margin_source),
        rows(margin_cell),
        rows(margin_weight),
    )
    ring = [(i, (i + 1) % tiles) for i in range(tiles)]
    mirror = lax.ppermute(mirror, "lon", [(i, tiles - 1 - i) for i in range(tiles)])
    west = lax.ppermute(up, "lon", ring)
    far = lax.ppermute(down, "lon", [(j, i) for i, j in ring])
    received = lax.all_to_all(messages, "lon", split_axis=0, concat_axis=0, tiled=True)
    out = step_columns(
        tracer,
        east,
        north,
        kappa,
        by_level(mixing),
        by_level(thickness),
        depth_levels,
        west,
        far,
        mirror,
        received,
    )
    return jnp.transpose(out, (0, 2, 1, 3))


def solution(mesh):
    placed = (
        P(None, "lon", None, "ens"),
        P("lon", None, "ens"),
        P("lon", None, "ens"),
        P("lon", None, "ens"),
        P("lon", None, "ens"),
        P("lon", None, "ens"),
        P("lon", "ens"),
        P("ens", "lon"),
        P(("ens", "lon"), None),
        P(("ens", "lon")),
        P(("ens", "lon")),
        P(("ens", "lon")),
    )
    return jax.shard_map(
        shards, mesh=mesh, in_specs=placed, out_specs=P(None, "lon", None, "ens"), check_vma=False
    )
```

time: 144 us -> 68.8 us (0.48)
  other arithmetic: 72.8 us -> 0 us
  Pallas kernels: 0 us -> 38.1 us
  local copies, waits for them, and re-layouts: 42 us -> 13.3 us
  starting transfers between devices: 20.3 us -> 13.5 us
  between operations: 2.83 us -> 0.06 us
    pallas_call x0 -> x2, Pallas kernels: none -> 38.1 us  [the longest x1 35.1 us: step_columns(): pl.pallas_call(functools.partial(step_kernel, levels), grid=(2 * blocks,)...]
    slice x20 -> x0, local copies, waits for them, and re-layouts: 15.2 us -> none  [the longest x2 4.85 us: shards(): tracer[:, :, :, -1]]
    mul x7 -> x0, other arithmetic: 12.9 us -> none  [the longest x3 6.84 us: face_flux(): open_face * (jnp.maximum(speed, 0.0) * near + jnp.minimum(speed, 0.0) * f...]
    sub x14 -> x0, other arithmetic: 12.6 us -> none  [the longest x13 9.39 us: mix_columns(): here_thickness + here_coupling + prior_coupling]
    unnamed x40 -> x0, other arithmetic: 10.3 us -> none
    scatter x1 -> x0, other arithmetic: 7.59 us -> none  [shards(): jnp.zeros((tracer_count, cycle_size * CAP), jnp.float32).at[:, position]]
    scatter-add x1 -> x0, other arithmetic: 7.4 us -> none  [shards(): surface = jnp.zeros((tracer_count, lon_cells * lat_cells), jnp.float32).a...]
    unnamed x349 -> x34, local copies, waits for them, and re-layouts: 7.9 us -> 13.3 us
  transfers between devices with their start and end apart: 8 -> 4, of which waited for: 2 -> 1; matrix products, arithmetic and copies ran while one was open for 54% -> 0% of each run, Pallas kernels for 0% -> 0%
where the time goes in v1:
time: 68.8 us; the launch traced here: 68.1 us
  Pallas kernels  38.1 us (55%)
  starting transfers between devices  13.5 us (20%)
  local copies, waits for them, and re-layouts  13.3 us (19%)
  waiting for transfers between devices  3.09 us (4%)
    pallas_call x1, Pallas kernels, step_columns(): pl.pallas_call(functools.partial(step_kernel, levels), grid=(2 * blocks,)...  35.1 us
    unnamed x34, local copies, waits for them, and re-layouts  13.3 us
    ppermute x1, starting transfers between devices, shards(): far = lax.ppermute(down, 'lon', [(j, i) for i, j in ring])  5 us
    ppermute x1, starting transfers between devices, shards(): lax.ppermute(mirror, 'lon', [(i, tiles - 1 - i) for i in range(tiles)])  4.38 us
    all_to_all x1, starting transfers between devices, shards(): lax.all_to_all(messages, 'lon', split_axis=0, concat_axis=0, tiled=True)  3.68 us
    ppermute x1, waiting for transfers between devices, shards(): lax.ppermute(mirror, 'lon', [(i, tiles - 1 - i) for i in range(tiles)])  3.08 us
    pallas_call x1, Pallas kernels, pack(): pl.pallas_call(functools.partial(pack_kernel, levels, tiles), grid=(level...  2.96 us
  transfers between devices with their start and end apart: 4, of which 1 were waited for; matrix products, arithmetic and copies ran while one was open for 0% of the time, Pallas kernels for 0%

profile of v1, /device:TPU:0, one launch (start us, length us, event | category | flops | bytes accessed | tf_op | source)
XLA Modules:
  0.0 68.1 jit_solution(9803358214870022666)
XLA Ops:
  0.0 0.0 copy-start.11
  0.0 0.0 copy-start
  0.0 1.7 %copy-done = f32[4,16,75,128]{3,1,2,0:T(8,128)S(1)} copy-done((f32[4,16,75,128]{3,1,2,0:T(8,128)S(1)}, f32[4,16,75,128]{3,1,2,0:T(8,128)}, u32[]{:S(2)}) %copy-start) | copy-done | bytes 2457624
  1.7 0.0 copy-start.2
  1.7 1.1 %copy-done.2 = f32[16,75,128]{2,0,1:T(8,128)S(1)} copy-done((f32[16,75,128]{2,0,1:T(8,128)S(1)}, f32[16,75,128]{2,0,1:T(8,128)}, u32[]{:S(2)}) %copy-start.2) | copy-done | bytes 614424
  2.8 0.0 copy-start.4
  2.8 1.1 %copy-done.4 = f32[16,75,128]{2,0,1:T(8,128)S(1)} copy-done((f32[16,75,128]{2,0,1:T(8,128)S(1)}, f32[16,75,128]{2,0,1:T(8,128)}, u32[]{:S(2)}) %copy-start.4) | copy-done | bytes 614424
  3.9 1.1 %copy-done.6 = f32[16,75,128]{2,0,1:T(8,128)S(1)} copy-done((f32[16,75,128]{2,0,1:T(8,128)S(1)}, f32[16,75,128]{2,0,1:T(8,128)}, u32[]{:S(2)}) %copy-start.6) | copy-done | bytes 614424
  4.9 0.7 %copy-done.10 = s32[16,128]{1,0:T(8,128)S(1)} copy-done((s32[16,128]{1,0:T(8,128)S(1)}, s32[16,128]{1,0:T(8,128)}, u32[]{:S(2)}) %copy-start.10) | copy-done | bytes 8216
  5.6 0.7 %copy-done.12 = f32[4,256]{1,0:T(4,128)S(1)} copy-done((f32[4,256]{1,0:T(4,128)S(1)}, f32[4,256]{1,0:T(4,128)}, u32[]{:S(2)}) %copy-start.12) | copy-done | bytes 4120
  6.3 0.7 %copy-done.13 = s32[1024,1]{0,1:T(1,128)S(1)} copy-done((s32[1024,1]{0,1:T(1,128)S(1)}, s32[1024,1]{0,1:T(1,128)}, u32[]{:S(2)}) %copy-start.13) | copy-done | bytes 4120
  7.0 0.7 %copy-done.14 = s32[1024]{0:T(1024)S(1)} copy-done((s32[1024]{0:T(1024)S(1)}, s32[1024]{0:T(1024)}, u32[]{:S(2)}) %copy-start.14) | copy-done | bytes 4120
  7.7 0.7 %copy-done.15 = s32[1024]{0:T(1024)S(1)} copy-done((s32[1024]{0:T(1024)S(1)}, s32[1024]{0:T(1024)}, u32[]{:S(2)}) %copy-start.15) | copy-done | bytes 4120
  8.4 0.7 %copy-done.16 = f32[1024]{0:T(1024)S(1)} copy-done((f32[1024]{0:T(1024)S(1)}, f32[1024]{0:T(1024)}, u32[]{:S(2)}) %copy-start.16) | copy-done | bytes 4120
  9.1 3.0 %pack.1 = (f32[456,128]{1,0:T(8,128)}, f32[376,128]{1,0:T(8,128)}, f32[96,128]{1,0:T(8,128)S(1)}, f32[16,8,128]{2,1,0:T(8,128)}) custom-call(f32[4,75,16,128]{3,2,1,0:T(8,128)S(1)} %bitcast.11, f32[75,16,128]{2,1,0:T(8,128)S(1)} %bitcast.13, f32[75,16,128]{2,1,0:T(8,128)S(1)} %bitcast.15, f32[75,16,128]{2,1,0:T(8,128)S(1)} %bitcast.17, ...), custom_call_target="tpu_custom_call" | custom-call | flops 10000000 | bytes 4000000 | tf_op jit(solution)/shard_map/pack/pallas_call | solution.py:181
  12.0 0.5 collective-permute-start
  12.5 5.0 %collective-permute-start.1 = (f32[376,128]{1,0:T(8,128)}, f32[376,128]{1,0:T(8,128)}, u32[]{:S(2)}, u32[]{:S(2)}) collective-permute-start(f32[376,128]{1,0:T(8,128)} %get-tuple-element.10), channel_id=1, source_target_pairs={{1,0},{2,1},{3,2},{4,3},{5,4},{6,5},{7,6},{8,7},{9,8},{10,9},{11,1... | collective-permute-start | bytes 577544 | tf_op jit(solution)/shard_map/ppermute | solution.py:479
  17.5 3.7 %all-to-all-start = ((f32[16,8,128]{2,1,0:T(8,128)}), f32[16,8,128]{2,1,0:T(8,128)S(1)}, u32[]{:S(2)}, u32[]{:S(2)}) async-start(f32[16,8,128]{2,1,0:T(8,128)} %get-tuple-element.12), calls=%async_computation | async-start | bytes 131072 | tf_op jit(solution)/shard_map/all_to_all | solution.py:480
  21.2 4.4 %collective-permute-start.2 = (f32[96,128]{1,0:T(8,128)S(1)}, f32[96,128]{1,0:T(8,128)S(1)}, u32[]{:S(2)}, u32[]{:S(2)}) collective-permute-start(f32[96,128]{1,0:T(8,128)S(1)} %get-tuple-element.11), channel_id=1, source_target_pairs={{0,15},{1,14},{2,13},{3,12},{4,11},{5,10},{6,9},{7,8},{8,7},{9,6},... | collective-permute-start | bytes 147464 | tf_op jit(solution)/shard_map/ppermute | solution.py:477
  25.6 3.1 %collective-permute-done.2.mirror_ref = f32[96,128]{1,0:T(8,128)S(1)} collective-permute-done((f32[96,128]{1,0:T(8,128)S(1)}, f32[96,128]{1,0:T(8,128)S(1)}, u32[]{:S(2)}, u32[]{:S(2)}) %collective-permute-start.2) | collective-permute-done | bytes 49184 | tf_op jit(solution)/shard_map/ppermute | solution.py:477
  28.6 0.0 all-to-all-done.received_ref
  28.6 0.0 collective-permute-done.1.far_ref
  28.6 0.0 collective-permute-done.west_ref
  28.7 0.0 copy-done.11
  28.7 0.0 copy-done.1
  28.7 0.0 copy-done.3
  28.7 0.0 copy-start.5
  28.7 1.1 %copy-done.5 = f32[16,75,128]{2,0,1:T(8,128)S(1)} copy-done((f32[16,75,128]{2,0,1:T(8,128)S(1)}, f32[16,75,128]{2,0,1:T(8,128)}, u32[]{:S(2)}) %copy-start.5) | copy-done | bytes 614424
  29.8 1.1 %copy-done.7 = f32[16,75,128]{2,0,1:T(8,128)S(1)} copy-done((f32[16,75,128]{2,0,1:T(8,128)S(1)}, f32[16,75,128]{2,0,1:T(8,128)}, u32[]{:S(2)}) %copy-start.7) | copy-done | bytes 614424
  30.8 1.1 %copy-done.8 = f32[16,75,128]{2,0,1:T(8,128)S(1)} copy-done((f32[16,75,128]{2,0,1:T(8,128)S(1)}, f32[16,75,128]{2,0,1:T(8,128)}, u32[]{:S(2)}) %copy-start.8) | copy-done | bytes 614424
  31.9 1.1 %copy-done.9 = f32[16,75,128]{2,0,1:T(8,128)S(1)} copy-done((f32[16,75,128]{2,0,1:T(8,128)S(1)}, f32[16,75,128]{2,0,1:T(8,128)}, u32[]{:S(2)}) %copy-start.9) | copy-done | bytes 614424
  33.0 35.1 %columns.1 = f32[4,75,16,128]{3,2,1,0:T(8,128)} custom-call(f32[4,75,16,128]{3,2,1,0:T(8,128)S(1)} %bitcast.12, f32[75,16,128]{2,1,0:T(8,128)S(1)} %bitcast.14, f32[75,16,128]{2,1,0:T(8,128)S(1)} %bitcast.16, f32[75,16,128]{2,1,0:T(8,128)S(1)} %bitcast.18, f32[75,16,128]{2,1,0:T(8,128)S(1)} %bitcast.19, f32[75,16,128]{2,1,0:T(8,128)S(1)} %bitcast.20, ...), custom_call_target="tpu_custom_call" | custom-call | flops 100000000 | bytes 8000000 | tf_op jit(solution)/shard_map/columns/pallas_call | solution.py:422
  (12 shorter events, 0.0 us)
Async XLA Ops:
  0.0 28.7 %copy-start.11 = (s32[16,128]{1,0:T(8,128)S(1)}, s32[16,128]{1,0:T(8,128)}, u32[]{:S(2)}) copy-start(s32[16,128]{1,0:T(8,128)} %depth_ref.3) | copy-start | bytes 24580
  0.0 1.7 %copy-start = (f32[4,16,75,128]{3,1,2,0:T(8,128)S(1)}, f32[4,16,75,128]{3,1,2,0:T(8,128)}, u32[]{:S(2)}) copy-start(f32[4,16,75,128]{3,1,2,0:T(8,128)} %param.12) | copy-start | bytes 7372804
  1.7 1.1 %copy-start.2 = (f32[16,75,128]{2,0,1:T(8,128)S(1)}, f32[16,75,128]{2,0,1:T(8,128)}, u32[]{:S(2)}) copy-start(f32[16,75,128]{2,0,1:T(8,128)} %param.13) | copy-start | bytes 1843204
  2.8 1.1 %copy-start.4 = (f32[16,75,128]{2,0,1:T(8,128)S(1)}, f32[16,75,128]{2,0,1:T(8,128)}, u32[]{:S(2)}) copy-start(f32[16,75,128]{2,0,1:T(8,128)} %param.14) | copy-start | bytes 1843204
  3.9 1.1 %copy-start.6 = (f32[16,75,128]{2,0,1:T(8,128)S(1)}, f32[16,75,128]{2,0,1:T(8,128)}, u32[]{:S(2)}) copy-start(f32[16,75,128]{2,0,1:T(8,128)} %param.15) | copy-start | bytes 1843204
  4.9 0.7 %copy-start.10 = (s32[16,128]{1,0:T(8,128)S(1)}, s32[16,128]{1,0:T(8,128)}, u32[]{:S(2)}) copy-start(s32[16,128]{1,0:T(8,128)} %depth_ref.3) | copy-start | bytes 24580
  5.6 0.7 %copy-start.12 = (f32[4,256]{1,0:T(4,128)S(1)}, f32[4,256]{1,0:T(4,128)}, u32[]{:S(2)}) copy-start(f32[4,256]{1,0:T(4,128)} %air_ref.1) | copy-start | bytes 12292
  6.3 0.7 %copy-start.13 = (s32[1024,1]{0,1:T(1,128)S(1)}, s32[1024,1]{0,1:T(1,128)}, u32[]{:S(2)}) copy-start(s32[1024,1]{0,1:T(1,128)} %param.20) | copy-start | bytes 12292
  7.0 0.7 %copy-start.14 = (s32[1024]{0:T(1024)S(1)}, s32[1024]{0:T(1024)}, u32[]{:S(2)}) copy-start(s32[1024]{0:T(1024)} %param.21) | copy-start | bytes 12292
  7.7 0.7 %copy-start.15 = (s32[1024]{0:T(1024)S(1)}, s32[1024]{0:T(1024)}, u32[]{:S(2)}) copy-start(s32[1024]{0:T(1024)} %param.22) | copy-start | bytes 12292
  8.4 0.7 %copy-start.16 = (f32[1024]{0:T(1024)S(1)}, f32[1024]{0:T(1024)}, u32[]{:S(2)}) copy-start(f32[1024]{0:T(1024)} %param.23) | copy-start | bytes 12292
  9.1 19.6 %copy-start.1 = (f32[4,16,75,128]{3,1,2,0:T(8,128)S(1)}, f32[4,16,75,128]{3,1,2,0:T(8,128)}, u32[]{:S(2)}) copy-start(f32[4,16,75,128]{3,1,2,0:T(8,128)} %param.12) | copy-start | bytes 7372804
  9.1 19.6 %copy-start.3 = (f32[16,75,128]{2,0,1:T(8,128)S(1)}, f32[16,75,128]{2,0,1:T(8,128)}, u32[]{:S(2)}) copy-start(f32[16,75,128]{2,0,1:T(8,128)} %param.13) | copy-start | bytes 1843204
  12.0 16.6 %collective-permute-start = (f32[456,128]{1,0:T(8,128)}, f32[456,128]{1,0:T(8,128)S(1)}, u32[]{:S(2)}, u32[]{:S(2)}) collective-permute-start(f32[456,128]{1,0:T(8,128)} %get-tuple-element.9), channel_id=1, source_target_pairs={{0,1},{1,2},{2,3},{3,4},{4,5},{5,6},{6,7},{7,8},{8,9},{9,10},{10,1... | collective-permute-start | bytes 700424 | tf_op jit(solution)/shard_map/ppermute | solution.py:478
  12.5 16.2 %collective-permute-start.1 = (f32[376,128]{1,0:T(8,128)}, f32[376,128]{1,0:T(8,128)}, u32[]{:S(2)}, u32[]{:S(2)}) collective-permute-start(f32[376,128]{1,0:T(8,128)} %get-tuple-element.10), channel_id=1, source_target_pairs={{1,0},{2,1},{3,2},{4,3},{5,4},{6,5},{7,6},{8,7},{9,8},{10,9},{11,1... | collective-permute-start | bytes 577544 | tf_op jit(solution)/shard_map/ppermute | solution.py:479
  17.5 11.2 %all-to-all-start = ((f32[16,8,128]{2,1,0:T(8,128)}), f32[16,8,128]{2,1,0:T(8,128)S(1)}, u32[]{:S(2)}, u32[]{:S(2)}) async-start(f32[16,8,128]{2,1,0:T(8,128)} %get-tuple-element.12), calls=%async_computation | async-start | bytes 131072 | tf_op jit(solution)/shard_map/all_to_all | solution.py:480
  21.2 7.5 %collective-permute-start.2 = (f32[96,128]{1,0:T(8,128)S(1)}, f32[96,128]{1,0:T(8,128)S(1)}, u32[]{:S(2)}, u32[]{:S(2)}) collective-permute-start(f32[96,128]{1,0:T(8,128)S(1)} %get-tuple-element.11), channel_id=1, source_target_pairs={{0,15},{1,14},{2,13},{3,12},{4,11},{5,10},{6,9},{7,8},{8,7},{9,6},... | collective-permute-start | bytes 147464 | tf_op jit(solution)/shard_map/ppermute | solution.py:477
  28.7 1.1 %copy-start.5 = (f32[16,75,128]{2,0,1:T(8,128)S(1)}, f32[16,75,128]{2,0,1:T(8,128)}, u32[]{:S(2)}) copy-start(f32[16,75,128]{2,0,1:T(8,128)} %param.14) | copy-start | bytes 1843204
  29.8 1.1 %copy-start.7 = (f32[16,75,128]{2,0,1:T(8,128)S(1)}, f32[16,75,128]{2,0,1:T(8,128)}, u32[]{:S(2)}) copy-start(f32[16,75,128]{2,0,1:T(8,128)} %param.15) | copy-start | bytes 1843204
  30.8 1.1 %copy-start.8 = (f32[16,75,128]{2,0,1:T(8,128)S(1)}, f32[16,75,128]{2,0,1:T(8,128)}, u32[]{:S(2)}) copy-start(f32[16,75,128]{2,0,1:T(8,128)} %param.16) | copy-start | bytes 1843204
  31.9 1.1 %copy-start.9 = (f32[16,75,128]{2,0,1:T(8,128)S(1)}, f32[16,75,128]{2,0,1:T(8,128)}, u32[]{:S(2)}) copy-start(f32[16,75,128]{2,0,1:T(8,128)} %param.17) | copy-start | bytes 1843204
